TPU v7x, 128 devices: a whole 4x4x4 slice. The times are simulated.
128 devices in a mesh: dp: 4 (over y_hi, core), row: 8 (over x, y_lo), col: 4 (over z).
Axes of the slice: x: 4, y: 4 (y_hi: 2, y_lo: 2; y = y_hi * 2 + y_lo), z: 4, core: 2. Of those that a mesh axis runs over, the one named last changes fastest.
Arguments:
- inputs: bfloat16 [2, 8192, 4096], P(None, ('dp', 'col'), 'row'), may hold values from -6 to 6
- out_grads: bfloat16 [4, 8192, 4096], P(None, ('dp', 'row'), 'col'), may hold values from -0.06629126 to 0.06629126
- weights: float32 [4, 4096, 4096], P(None, 'row', 'col'), may hold values from -2 to 2
- row_moment: float32 [4, 4096], P(None, 'row'), may hold values from 0.01 to 1
- col_moment: float32 [4, 4096], P(None, 'col'), may hold values from 0.1 to 1
Outputs:
- weight_change: float32 [4, 4096, 4096], P(None, 'row', 'col')
- new_row: float32 [4, 4096], P(None, 'row')
- new_col: float32 [4, 4096], P(None, 'col')
All inputs are finite; a program needn't handle non-finite values.
Results may differ from a plain program's by a relative error of at most 0.0003.
Values may be sent and summed in bfloat16 or wider, within the bound.
A program may use at most 128 MiB of HBM per device.

v0:
```python
import jax
import jax.numpy as jnp
from jax import lax
from jax.sharding import PartitionSpec as P

D = 4096
STEP = 10


def local(inputs, out_grads, weights, row_moment, col_moment):
    decay_rate = 1.0 - float(STEP) ** (-0.8)
    relative = min(0.01, float(STEP) ** (-0.5))
    activations = lax.all_gather(inputs, "col", axis=1, tiled=True)
    piece = lax.all_gather(out_grads, "row", axis=1, tiled=True)
    shared = jnp.einsum(
        "tr,ptc->prc", activations[0], piece[:3], preferred_element_type=jnp.float32
    )
    output_part = jnp.einsum(
        "tr,tc->rc", activations[1], piece[3], preferred_element_type=jnp.float32
    )
    partial_grad = jnp.concatenate([shared, output_part[None]], 0)
    gradient = lax.psum(partial_grad, "dp")
    squares = gradient * gradient + 1e-30
    row_part = jnp.sum(squares, 2)
    col_part = jnp.sum(squares, 1)
    param_part = jnp.sum(weights * weights, (1, 2))
    row_sums = lax.psum(row_part, "col")
    row_new = decay_rate * row_moment + (1.0 - decay_rate) * (row_sums / D)
    col_sums = lax.psum(col_part, "row")
    row_total = lax.psum(jnp.sum(row_new, 1), "row")
    param_total = lax.psum(param_part, ("row", "col"))
    col_new = decay_rate * col_moment + (1.0 - decay_rate) * (col_sums / D)
    mean_row = row_total / D
    update = gradient * lax.rsqrt(
        row_new[:, :, None] * col_new[:, None, :] / mean_row[:, None, None]
    )
    update_part = jnp.sum(update * update, (1, 2))
    update_total = lax.psum(update_part, ("row", "col"))
    clip_factor = jnp.maximum(1.0, jnp.sqrt(update_total / (D * D)))
    step_size = relative * jnp.maximum(0.001, jnp.sqrt(param_total / (D * D)))
    change = -(step_size / clip_factor)[:, None, None] * update
    return (change, row_new, col_new)


def solution(mesh):
    return jax.shard_map(
        local,
        mesh=mesh,
        in_specs=(
            P(None, ("dp", "col"), "row"),
            P(None, ("dp", "row"), "col"),
            P(None, "row", "col"),
            P(None, "row"),
            P(None, "col"),
        ),
        out_specs=(P(None, "row", "col"), P(None, "row"), P(None, "col")),
        check_vma=False,
    )
```

profile of v0, /device:TPU:0, one launch (start us, length us, event | category | flops | bytes accessed | tf_op | source)
XLA Modules:
  0.0 723.4 jit_solution(2207020887193942174)
XLA Ops:
  7.2 0.0 all-gather.5.cloned.1.call-start
  7.2 0.7 all-gather.5.cloned.1.call-update
  7.9 0.0 all-gather.3.cloned.1.call-start
  7.9 3.9 copy.8
  11.9 0.0 all-gather.3.cloned.1.call-update
  11.9 0.0 all-reduce.4.cloned.1.call-start
  12.0 48.7 %all-gather.5.cloned.1.call-done = bf16[2,2048,512]{2,1,0:T(8,128)(2,1)} async-done(((bf16[2,512,512]{2,1,0:T(8,128)(2,1)}), bf16[2,2048,512]{2,1,0:T(8,128)(2,1)}) %all-gather.5.cloned.1.call-update) | async-done | bytes 4194320 | tf_op jit(solution)/shard_map/all_gather | solution.py:13
  60.6 329.0 %all-gather.3.cloned.1.call-done = bf16[4,2048,1024]{1,2,0:T(8,128)(2,1)} async-done(((bf16[4,256,1024]{1,2,0:T(8,128)(2,1)}), bf16[4,2048,1024]{1,2,0:T(8,128)(2,1)}) %all-gather.3.cloned.1.call-update) | async-done | bytes 16777232 | tf_op jit(solution)/shard_map/all_gather | solution.py:14
  389.7 0.0 copy-start.4
  389.7 10.8 %convolution_bitcast_fusion = f32[3,512,1024]{1,2,0:T(8,128)S(1)} fusion(bf16[4,2048,1024]{1,2,0:T(8,128)(2,1)} %all-gather.3.cloned.1.call-done, bf16[2,2048,512]{2,1,0:T(8,128)(2,1)} %all-gather.5.cloned.1.call-done), kind=kOutput, calls=%fused_computation.10 | convolution fusion | flops 6442450944 | bytes 25165824 | tf_op jit(solution)/shard_map/tr,ptc->prc/dot_general | solution.py:15
  400.5 0.0 copy-done.4
  400.5 4.5 fusion.3
  405.0 4.4 pad_maximum_fusion
  409.4 0.0 all-reduce.4.cloned.1.call-update
  409.4 0.0 copy-start.3
  409.4 0.0 copy-start.2
  409.5 4.2 multiply_reduce_fusion.1
  413.7 157.8 %all-reduce.4.cloned.1.call-done = f32[4,512,1024]{1,2,0:T(8,128)} async-done(((f32[4,512,1024]{1,2,0:T(8,128)}), f32[4,512,1024]{1,2,0:T(8,128)}) %all-reduce.4.cloned.1.call-update) | async-done | bytes 8388624 | tf_op jit(solution)/shard_map/psum | solution.py:22
  571.5 4.8 fusion
  576.3 10.8 %psum.44 = f32[4,512]{1,0:T(4,128)S(1)} all-reduce(f32[4,512]{1,0:T(4,128)S(1)} %get-tuple-element.7), channel_id=1, replica_groups=mesh['dp'=4,'row'=8,'col'=4] {'col'}, use_global_device_ids=true, to_apply=%region_4.0 | all-reduce | flops 2048 | bytes 16384 | tf_op jit(solution)/shard_map/psum | solution.py:27
  587.1 0.0 copy-done.3
  587.1 0.1 fusion.5
  587.2 0.0 copy-start.1
  587.2 33.2 %all-reduce.1 = (f32[4]{0:T(128)S(1)}, f32[4,1024]{1,0:T(4,128)S(1)}) all-reduce(f32[4]{0:T(128)S(1)} %get-tuple-element.12, f32[4,1024]{1,0:T(4,128)S(1)} %get-tuple-element.6), channel_id=1, replica_groups=mesh['dp'=4,'row'=8,'col'=4] {'row'}, use_global_device_ids=true, to_apply=%region_8.0 | all-reduce | flops 4100 | bytes 32800 | tf_op jit(solution)/shard_map/psum | solution.py:30
  620.4 0.0 copy-done.2
  620.5 0.0 copy-start
  620.5 4.7 multiply_reduce_fusion
  625.2 76.8 %all-reduce = (f32[4]{0:T(128)S(1)}, f32[4]{0:T(128)S(1)}) all-reduce(f32[4]{0:T(128)S(1)} %multiply_reduce_fusion, f32[4]{0:T(128)S(1)} %multiply_reduce_fusion.1), channel_id=1, replica_groups=mesh['dp'=4,'row'=8,'col'=4] {'row','col'}, use_global_device_ids=true, to_apply=%region_10.0 | all-reduce | flops 8 | bytes 64 | tf_op jit(solution)/shard_map/psum | solution.py:38
  702.0 6.2 broadcast_multiply_fusion
  708.2 0.0 copy-done.1
  708.2 0.0 copy-done
  708.2 8.7 %copy.10 = f32[4,512,1024]{2,1,0:T(8,128)} copy(f32[4,512,1024]{1,2,0:T(8,128)} %broadcast_multiply_fusion) | data formatting | bytes 16777216
  (3 shorter events, 0.0 us)
Async XLA Ops:
  7.2 53.5 %all-gather.5.cloned.1.call-start = ((), (), s32[]{:S(2)}) async-start(), calls=%async_computation.1 | async-start | bytes 5242880 | tf_op jit(solution)/shard_map/all_gather | solution.py:13
  7.9 381.8 %all-gather.3.cloned.1.call-start = ((), (), s32[]{:S(2)}) async-start(), calls=%async_computation | async-start | bytes 18874368 | tf_op jit(solution)/shard_map/all_gather | solution.py:14
  11.9 559.6 %all-reduce.4.cloned.1.call-start = ((), (), s32[]{:S(2)}) async-start(), calls=%async_computation.2 | async-start | bytes 16777216 | tf_op jit(solution)/shard_map/psum | solution.py:22
  389.7 10.8 %copy-start.4 = (bf16[2,2048,512]{2,1,0:T(8,128)(2,1)S(1)}, bf16[2,2048,512]{2,1,0:T(8,128)(2,1)}, u32[]{:S(2)}) copy-start(bf16[2,2048,512]{2,1,0:T(8,128)(2,1)} %all-gather.5.cloned.1.call-done) | copy-start | bytes 12582916
  409.4 177.7 %copy-start.3 = (f32[4,512]{1,0:T(4,128)S(1)}, f32[4,512]{1,0:T(4,128)}, u32[]{:S(2)}) copy-start(f32[4,512]{1,0:T(4,128)} %param.8) | copy-start | bytes 24580
  409.4 211.0 %copy-start.2 = (f32[4,1024]{1,0:T(4,128)S(1)}, f32[4,1024]{1,0:T(4,128)}, u32[]{:S(2)}) copy-start(f32[4,1024]{1,0:T(4,128)} %param.9) | copy-start | bytes 49156
  587.2 121.0 %copy-start.1 = (f32[4,512]{1,0:T(4,128)}, f32[4,512]{1,0:T(4,128)S(1)}, u32[]{:S(2)}) copy-start(f32[4,512]{1,0:T(4,128)S(1)} %get-tuple-element.13) | copy-start | bytes 24580
  620.5 87.8 %copy-start = (f32[4,1024]{1,0:T(4,128)}, f32[4,1024]{1,0:T(4,128)S(1)}, u32[]{:S(2)}) copy-start(f32[4,1024]{1,0:T(4,128)S(1)} %multiply_add_fusion.1) | copy-start | bytes 49156
Sparse Core Ops, SparseCore 0:
  9.7 50.9 all-gather.4
  62.8 326.8 all-gather.2
  409.6 161.9 all-reduce.3
where the time goes:
time: 724 us; the launch traced here: 723 us
  waiting for transfers between devices  536 us (74%)
  blocking collectives  121 us (17%)
  other arithmetic  24.5 us (3%)
  matrix products  15.3 us (2%)
  between operations  13.8 us (2%)
  local copies, waits for them, and re-layouts  12.6 us (2%)
    all_gather x1, waiting for transfers between devices, local(): piece = lax.all_gather(out_grads, 'row', axis=1, tiled=True)  329 us
    psum x1, waiting for transfers between devices, local(): gradient = lax.psum(partial_grad, 'dp')  158 us
    psum x1, blocking collectives, local(): update_total = lax.psum(update_part, ('row', 'col'))  76.8 us
    all_gather x1, waiting for transfers between devices, local(): activations = lax.all_gather(inputs, 'col', axis=1, tiled=True)  48.7 us
    psum x1, blocking collectives, local(): row_total = lax.psum(jnp.sum(row_new, 1), 'row')  33.2 us
  transfers between devices with their start and end apart: 3, of which 3 were waited for; matrix products, arithmetic and copies ran while one was open for 1% of the time, Pallas kernels for 0%

commit v1 on v0

--- a/solution.py
+++ b/solution.py
@@ -1,25 +1,264 @@
 import jax
 import jax.numpy as jnp
 from jax import lax
+from jax.experimental import pallas as pl
+from jax.experimental.pallas import tpu as pltpu
 from jax.sharding import PartitionSpec as P
 
 D = 4096
 STEP = 10
+MESH = pl.DeviceIdType.MESH
+TOK = 256
+HALF = 512
+
+
+def gradient_kernel(
+    inputs, out_grads, out, lbuf, rbuf, part, core_in, pair_in, final,
+    s_loc, s_ly, r_ly, s_ry, r_ry, s_xa, r_xa, s_xb, r_xb, s_xf, r_xf,
+    s_z, r_z, s_zf, r_zf, s_core, r_core, s_pair, r_pair, s_gc, r_gc, s_gy, r_gy, s_gf, r_gf, s_out,
+):
+    dp, row, z = lax.axis_index("dp"), lax.axis_index("row"), lax.axis_index("col")
+    yh, c, x, yl = dp // 2, dp % 2, row // 2, row % 2
+
+    def device(dx=0, m=0, dz=0, other=False):
+        h = 1 - yh if m & 2 else yh
+        l = 1 - yl if m & 1 else yl
+        return {
+            "dp": h * 2 + (1 - c if other else c),
+            "row": ((x + dx) % 4) * 2 + l,
+            "col": (z + dz) % 4,
+        }
+
+    def send(src, dst, ss, rs, to):
+        copy = pltpu.make_async_remote_copy(
+            src_ref=src, dst_ref=dst, send_sem=ss, recv_sem=rs, device_id=to, device_id_type=MESH
+        )
+        copy.start()
+        sent.append(copy)
+        return copy
+
+    sent = []
+    neighbours = [device(dx=1), device(dx=-1), device(dz=1), device(dz=-1),
+                  device(m=1), device(m=2), device(m=3), device(other=True)]
+    barrier = pltpu.get_barrier_semaphore()
+    for other in neighbours:
+        pl.semaphore_signal(barrier, inc=1, device_id=other, device_id_type=MESH)
+    pl.semaphore_wait(barrier, len(neighbours))
+
+    def flip(bit, value):
+        return 1 - value if bit else value
+
+    def token_rows(m):
+        h = yl
+        if (m >> 1) ^ (m & 1):
+            h = 1 - yl
+        return pl.ds(pl.multiple_of(h * TOK, TOK), TOK)
+
+    def columns(h):
+        return pl.ds(pl.multiple_of(h * HALF, HALF), HALF)
+
+    def l_part(s, m, dz=0):
+        return lbuf.at[s, flip(m & 1, yl), (z + dz) % 4, flip(m & 2, yh)]
+
+    def r_part(p, m, dx=0):
+        return rbuf.at[p, (x + dx) % 4, flip(m, yh)]
+
+    local = []
+    for s in range(2):
+        copy = pltpu.make_async_copy(inputs.at[s, token_rows(0), :], l_part(s, 0), s_loc.at[s])
+        copy.start()
+        local.append(copy)
+    for p in range(4):
+        copy = pltpu.make_async_copy(out_grads.at[p, :, columns(yh)], r_part(p, 0), s_loc.at[2 + p])
+        copy.start()
+        local.append(copy)
+
+    ly, ry, xa, xb, xf, zz, zf = {}, {}, {}, {}, {}, {}, {}
+
+    def send_ly(s, m):
+        ly[s, m] = send(inputs.at[s, token_rows(m), :], l_part(s, 0), s_ly.at[s, m - 1], r_ly.at[s, m - 1], device(m=m))
+
+    def send_ry(p):
+        ry[p] = send(out_grads.at[p, :, columns(1 - yh)], r_part(p, 0), s_ry.at[p], r_ry.at[p], device(m=3))
+
+    def send_xa(p):
+        for d in range(2):
+            xa[p, d] = send(out_grads.at[p, :, columns(yh)], r_part(p, 0), s_xa.at[p, d], r_xa.at[p, d], device(dx=1 - 2 * d))
+
+    def send_xb(p):
+        ry[p].wait_recv()
+        for d in range(2):
+            xb[p, d] = send(r_part(p, 1), r_part(p, 1), s_xb.at[p, d], r_xb.at[p, d], device(dx=1 - 2 * d))
+
+    def send_xf(p):
+        xa[p, 0].wait_recv()
+        xf[p, 0] = send(r_part(p, 0, -1), r_part(p, 0, -1), s_xf.at[p, 0], r_xf.at[p, 0], device(dx=1))
+        xb[p, 1].wait_recv()
+        xf[p, 1] = send(r_part(p, 1, 1), r_part(p, 1, 1), s_xf.at[p, 1], r_xf.at[p, 1], device(dx=-1))
+
+    def send_z(s, m):
+        if m:
+            ly[s, m].wait_recv()
+        for d in range(2):
+            src = l_part(s, m) if m else inputs.at[s, token_rows(0), :]
+            zz[s, m, d] = send(src, l_part(s, m), s_z.at[s, m, d], r_z.at[s, m, d], device(dz=1 - 2 * d))
+
+    def send_zf(s, m):
+        d = m // 2
+        back = 2 * d - 1
+        zz[s, m, d].wait_recv()
+        zf[s, m] = send(l_part(s, m, back), l_part(s, m, back), s_zf.at[s, m], r_zf.at[s, m], device(dz=-back))
+
+    core, pair, to_core, to_y, fwd, outs = {}, {}, {}, {}, {}, []
+    mine = pl.ds(pl.multiple_of(c * TOK, TOK), TOK)
+    theirs = pl.ds(pl.multiple_of((1 - c) * TOK, TOK), TOK)
+
+    def wait_r(p):
+        local[2 + p].wait()
+        for d in range(2):
+            if d == 1:
+                xa[p, d].wait_recv()
+            else:
+                xb[p, d].wait_recv()
+            xf[p, d].wait_recv()
+
+    def wait_l(s):
+        local[s].wait()
+        for m in range(4):
+            zz[s, m, 1 - m // 2].wait_recv()
+            zf[s, m].wait_recv()
+
+    def compute(p):
+        s = 0 if p < 3 else 1
+        for l in range(2):
+            right = rbuf[p].reshape(8 * TOK, HALF)
+
+            def rows(rs):
+                left = lbuf[s, l, :, :, :, rs].reshape(8 * TOK, TOK)
+                part[p, l, rs, :] = lax.dot_general(
+                    left, right, (((0,), (0,)), ((), ())), preferred_element_type=jnp.float32
+                )
+
+            rows(theirs)
+            core[p, l] = send(
+                part.at[p, l, theirs, :], core_in.at[p, l], s_core.at[p, l], r_core.at[p, l], device(other=True)
+            )
+            rows(mine)
+
+    def reduce_cores(p):
+        for l in range(2):
+            core[p, l].wait_recv()
+            part[p, l, mine, :] += core_in[p, l]
+        pair[p] = send(part.at[p, 1 - yl, mine, :], pair_in.at[p], s_pair.at[p], r_pair.at[p], device(m=1))
+
+    def finish(p):
+        pair[p].wait_recv()
+        final[p] = part[p, yl, mine, :] + pair_in[p]
+        here = out.at[p, mine, columns(yh)]
+        to_y[p] = send(final.at[p], here, s_gy.at[p], r_gy.at[p], device(m=2))
+        to_core[p] = send(final.at[p], here, s_gc.at[p], r_gc.at[p], device(other=True))
+        copy = pltpu.make_async_copy(final.at[p], here, s_out.at[p])
+        copy.start()
+        outs.append(copy)
+
+    def forward(p):
+        to_y[p].wait_recv()
+        there = out.at[p, mine, columns(1 - yh)]
+        fwd[p] = send(there, there, s_gf.at[p], r_gf.at[p], device(other=True))
+
+    send_ry(0)
+    for m in (1, 3, 2):
+        send_ly(0, m)
+    send_xa(0)
+    send_z(0, 0)
+    send_ry(1)
+    send_z(1, 0)
+    for m in (1, 3, 2):
+        send_ly(1, m)
+    send_ry(2)
+    send_ry(3)
+    send_xb(0)
+    send_xa(1)
+    for m in (1, 3, 2):
+        send_z(0, m)
+    send_xf(0)
+    send_xb(1)
+    send_xa(2)
+    for m in (0, 1, 3, 2):
+        send_zf(0, m)
+    send_xf(1)
+    send_xb(2)
+    send_xa(3)
+    for m in (1, 3, 2):
+        send_z(1, m)
+    wait_l(0)
+    wait_r(0)
+    compute(0)
+    wait_r(1)
+    compute(1)
+    reduce_cores(0)
+    reduce_cores(1)
+    send_xf(2)
+    send_xb(3)
+    for m in (0, 1, 3, 2):
+        send_zf(1, m)
+    finish(0)
+    wait_r(2)
+    compute(2)
+    send_xf(3)
+    reduce_cores(2)
+    finish(1)
+    wait_l(1)
+    wait_r(3)
+    compute(3)
+    reduce_cores(3)
+    forward(0)
+    finish(2)
+    forward(1)
+    finish(3)
+    forward(2)
+    forward(3)
+    for p in range(4):
+        to_core[p].wait_recv()
+        fwd[p].wait_recv()
+        outs[p].wait()
+    for copy in sent:
+        copy.wait_send()
+
+
+def gradients(inputs, out_grads):
+    dma = pltpu.SemaphoreType.DMA
+    any_space = pl.BlockSpec(memory_space=pl.ANY)
+    return pl.pallas_call(
+        gradient_kernel,
+        out_shape=jax.ShapeDtypeStruct((4, 512, 1024), jnp.float32),
+        in_specs=[any_space, any_space],
+        out_specs=any_space,
+        scratch_shapes=[
+            pltpu.VMEM((2, 2, 4, 2, TOK, HALF), jnp.bfloat16),
+            pltpu.VMEM((4, 4, 2, TOK, HALF), jnp.bfloat16),
+            pltpu.VMEM((4, 2, 512, HALF), jnp.float32),
+            pltpu.VMEM((4, 2, TOK, HALF), jnp.float32),
+            pltpu.VMEM((4, TOK, HALF), jnp.float32),
+            pltpu.VMEM((4, TOK, HALF), jnp.float32),
+            dma((6,)),
+            dma((2, 3)), dma((2, 3)), dma((4,)), dma((4,)),
+            dma((4, 2)), dma((4, 2)), dma((4, 2)), dma((4, 2)), dma((4, 2)), dma((4, 2)),
+            dma((2, 4, 2)), dma((2, 4, 2)), dma((2, 4)), dma((2, 4)),
+            dma((4, 2)), dma((4, 2)), dma((4,)), dma((4,)),
+            dma((4,)), dma((4,)), dma((4,)), dma((4,)), dma((4,)), dma((4,)), dma((4,)),
+        ],
+        name="gradients",
+        compiler_params=pltpu.CompilerParams(
+            collective_id=0, has_side_effects=True, vmem_limit_bytes=56 * 2**20
+        ),
+    )(inputs, out_grads)
 
 
 def local(inputs, out_grads, weights, row_moment, col_moment):
     decay_rate = 1.0 - float(STEP) ** (-0.8)
     relative = min(0.01, float(STEP) ** (-0.5))
-    activations = lax.all_gather(inputs, "col", axis=1, tiled=True)
-    piece = lax.all_gather(out_grads, "row", axis=1, tiled=True)
-    shared = jnp.einsum(
-        "tr,ptc->prc", activations[0], piece[:3], preferred_element_type=jnp.float32
-    )
-    output_part = jnp.einsum(
-        "tr,tc->rc", activations[1], piece[3], preferred_element_type=jnp.float32
-    )
-    partial_grad = jnp.concatenate([shared, output_part[None]], 0)
-    gradient = lax.psum(partial_grad, "dp")
+    gradient = gradients(inputs, out_grads)
     squares = gradient * gradient + 1e-30
     row_part = jnp.sum(squares, 2)
     col_part = jnp.sum(squares, 1)

time: 724 us -> 296 us (0.41)
  waiting for transfers between devices: 536 us -> 0 us
  Pallas kernels: 0 us -> 154 us
  matrix products: 15.3 us -> 0 us
  between operations: 13.8 us -> 0.71 us
  local copies, waits for them, and re-layouts: 12.6 us -> 0.02 us
    all_gather x2 -> x0, waiting for transfers between devices: 378 us -> none  [the longest x1 329 us: local(): piece = lax.all_gather(out_grads, 'row', axis=1, tiled=True)]
    psum x1 -> x0, waiting for transfers between devices: 158 us -> none  [local(): gradient = lax.psum(partial_grad, 'dp')]
    pallas_call x0 -> x1, Pallas kernels: none -> 154 us  [gradients(): pl.pallas_call(gradient_kernel, out_shape=jax.ShapeDtypeStruct((4, 512, 1...]
    dot_general x2 -> x0, matrix products: 15.3 us -> none  [the longest x1 10.8 us: local(): jnp.einsum('tr,ptc->prc', activations[0], piece[:3], preferred_element_ty...]
    unnamed x12 -> x8, local copies, waits for them, and re-layouts: 12.6 us -> 0.02 us
  transfers between devices with their start and end apart: 3 -> 0, of which waited for: 3 -> 0; matrix products, arithmetic and copies ran while one was open for 1% -> 0% of each run, Pallas kernels for 0% -> 0%
where the time goes in v1:
time: 296 us
  Pallas kernels  154 us (52%)
  blocking collectives  120 us (41%)
  other arithmetic  20.2 us (7%)
    pallas_call x1, Pallas kernels, gradients(): pl.pallas_call(gradient_kernel, out_shape=jax.ShapeDtypeStruct((4, 512, 1...  154 us
    psum x1, blocking collectives, local(): update_total = lax.psum(update_part, ('row', 'col'))  78.4 us
    psum x1, blocking collectives, local(): row_total = lax.psum(jnp.sum(row_new, 1), 'row')  33.5 us
    psum x1, blocking collectives, local(): row_sums = lax.psum(row_part, 'col')  8.33 us
    mul x1, other arithmetic, local(): change = -(step_size / clip_factor)[:, None, None] * update  6.34 us

profile of v1, /device:TPU:0, one launch (start us, length us, event | category | flops | bytes accessed | tf_op | source)
XLA Modules:
  0.0 295.6 jit_solution(14684226066291313814)
XLA Ops:
  0.6 0.0 copy-start.3
  0.6 0.0 copy-start.2
  0.7 154.4 %gradients.1 = f32[4,512,1024]{2,1,0:T(8,128)} custom-call(bf16[2,512,512]{2,1,0:T(8,128)(2,1)} %inputs.1, bf16[4,256,1024]{2,1,0:T(8,128)(2,1)} %out_grads.1), custom_call_target="tpu_custom_call" | custom-call | tf_op jit(solution)/shard_map/gradients/pallas_call | solution.py:232
  155.0 4.8 %fusion = (f32[4,1024]{1,0:T(4,128)S(1)}, f32[4,512]{1,0:T(4,128)S(1)}) fusion(f32[4,512,1024]{2,1,0:T(8,128)} %gradients.1), kind=kLoop, calls=%fused_computation.4 | loop fusion | flops 8382464 | bytes 8413184 | tf_op jit(solution)/shard_map/reduce_sum | solution.py:264
  159.8 8.3 %psum.36 = f32[4,512]{1,0:T(4,128)S(1)} all-reduce(f32[4,512]{1,0:T(4,128)S(1)} %get-tuple-element.4), channel_id=1, replica_groups=mesh['dp'=4,'row'=8,'col'=4] {'col'}, use_global_device_ids=true, to_apply=%region_3.0 | all-reduce | flops 2048 | bytes 16384 | tf_op jit(solution)/shard_map/psum | solution.py:266
  168.1 0.0 copy-done.3
  168.2 0.1 fusion.3
  168.3 0.0 copy-start.1
  168.3 33.5 %all-reduce.1 = (f32[4]{0:T(128)S(1)}, f32[4,1024]{1,0:T(4,128)S(1)}) all-reduce(f32[4]{0:T(128)S(1)} %get-tuple-element.9, f32[4,1024]{1,0:T(4,128)S(1)} %get-tuple-element.3), channel_id=1, replica_groups=mesh['dp'=4,'row'=8,'col'=4] {'row'}, use_global_device_ids=true, to_apply=%region_7.0 | all-reduce | flops 4100 | bytes 32800 | tf_op jit(solution)/shard_map/psum | solution.py:269
  201.8 0.0 copy-done.2
  201.8 0.0 copy-start
  201.9 4.7 %multiply_reduce_fusion = f32[4]{0:T(128)S(1)} fusion(f32[4,512,1024]{2,1,0:T(8,128)} %gradients.1, f32[4]{0:T(128)S(1)} %broadcast_multiply_fusion.1, f32[4,1024]{1,0:T(4,128)S(1)} %multiply_add_fusion.1, f32[4,512]{1,0:T(4,128)S(1)} %get-tuple-element.10), kind=kLoop, calls=%fused_computation | loop fusion | flops 10485756 | bytes 8413216 | tf_op jit(solution)/shard_map/reduce_sum | solution.py:276
  206.5 4.2 %multiply_reduce_fusion.1 = f32[4]{0:T(128)S(1)} fusion(f32[4,512,1024]{2,1,0:T(8,128)} %param.7), kind=kLoop, calls=%fused_computation.3 | loop fusion | flops 4194300 | bytes 8388624 | tf_op jit(solution)/shard_map/reduce_sum | solution.py:265
  210.8 78.4 %all-reduce = (f32[4]{0:T(128)S(1)}, f32[4]{0:T(128)S(1)}) all-reduce(f32[4]{0:T(128)S(1)} %multiply_reduce_fusion, f32[4]{0:T(128)S(1)} %multiply_reduce_fusion.1), channel_id=1, replica_groups=mesh['dp'=4,'row'=8,'col'=4] {'row','col'}, use_global_device_ids=true, to_apply=%region_9.0 | all-reduce | flops 8 | bytes 64 | tf_op jit(solution)/shard_map/psum | solution.py:277
  289.2 0.0 copy-done.1
  289.2 0.0 copy-done
  289.2 6.3 %broadcast_multiply_fusion = f32[4,512,1024]{2,1,0:T(8,128)} fusion(f32[4]{0:T(128)S(1)} %fusion.2, f32[4,512,1024]{2,1,0:T(8,128)} %gradients.1, f32[4]{0:T(128)S(1)} %broadcast_multiply_fusion.1, f32[4,1024]{1,0:T(4,128)S(1)} %multiply_add_fusion.1, f32[4,512]{1,0:T(4,128)S(1)} %get-tuple-element.10), kind=kLoop, calls=%fused_computation.6 | loop fusion | flops 8388608 | bytes 16801824 | tf_op jit(solution)/shard_map/mul | solution.py:280
  (3 shorter events, 0.0 us)
Async XLA Ops:
  0.6 167.5 %copy-start.3 = (f32[4,512]{1,0:T(4,128)S(1)}, f32[4,512]{1,0:T(4,128)}, u32[]{:S(2)}) copy-start(f32[4,512]{1,0:T(4,128)} %param.8) | copy-start | bytes 24580
  0.6 201.2 %copy-start.2 = (f32[4,1024]{1,0:T(4,128)S(1)}, f32[4,1024]{1,0:T(4,128)}, u32[]{:S(2)}) copy-start(f32[4,1024]{1,0:T(4,128)} %param.9) | copy-start | bytes 49156
  168.3 120.9 %copy-start.1 = (f32[4,512]{1,0:T(4,128)}, f32[4,512]{1,0:T(4,128)S(1)}, u32[]{:S(2)}) copy-start(f32[4,512]{1,0:T(4,128)S(1)} %get-tuple-element.10) | copy-start | bytes 24580
  201.8 87.4 %copy-start = (f32[4,1024]{1,0:T(4,128)}, f32[4,1024]{1,0:T(4,128)S(1)}, u32[]{:S(2)}) copy-start(f32[4,1024]{1,0:T(4,128)S(1)} %multiply_add_fusion.1) | copy-start | bytes 49156

commit v2 on v1

--- a/solution.py
+++ b/solution.py
@@ -13,9 +13,11 @@
 
 
 def gradient_kernel(
-    inputs, out_grads, out, lbuf, rbuf, part, core_in, pair_in, final,
+    inputs, out_grads, weights, row_moment, col_moment, out, out_row, out_col, out_left, out_right,
+    lbuf, rbuf, part, core_in, pair_in, final, share, rowx, colx, rown, coln, sum1, sum2,
     s_loc, s_ly, r_ly, s_ry, r_ry, s_xa, r_xa, s_xb, r_xb, s_xf, r_xf,
     s_z, r_z, s_zf, r_zf, s_core, r_core, s_pair, r_pair, s_gc, r_gc, s_gy, r_gy, s_gf, r_gf, s_out,
+    s_share, s_rx, r_rx, s_cx, r_cx, s_rn, r_rn, s_cn, r_cn, s_s1, r_s1, s_s2, r_s2,
 ):
     dp, row, z = lax.axis_index("dp"), lax.axis_index("row"), lax.axis_index("col")
     yh, c, x, yl = dp // 2, dp % 2, row // 2, row % 2
@@ -38,8 +40,12 @@
         return copy
 
     sent = []
-    neighbours = [device(dx=1), device(dx=-1), device(dz=1), device(dz=-1),
-                  device(m=1), device(m=2), device(m=3), device(other=True)]
+    row_peers = [(dz * 2 + h, device(dz=dz, m=2 * h)) for dz in range(4) for h in range(2) if dz + h]
+    col_peers = [
+        (dx * 4 + l * 2 + o, device(dx=dx, m=l, other=bool(o)))
+        for dx in range(4) for l in range(2) for o in range(2) if dx + l + o
+    ]
+    neighbours = [to for _, to in row_peers + col_peers] + [device(m=3)]
     barrier = pltpu.get_barrier_semaphore()
     for other in neighbours:
         pl.semaphore_signal(barrier, inc=1, device_id=other, device_id_type=MESH)
@@ -63,6 +69,8 @@
     def r_part(p, m, dx=0):
         return rbuf.at[p, (x + dx) % 4, flip(m, yh)]
 
+    quarter = pl.ds(pl.multiple_of(dp * 128, 128), 128)
+    own_weights = pltpu.make_async_copy(weights.at[:, quarter, :], share, s_share.at[0])
     local = []
     for s in range(2):
         copy = pltpu.make_async_copy(inputs.at[s, token_rows(0), :], l_part(s, 0), s_loc.at[s])
@@ -151,9 +159,46 @@
             part[p, l, mine, :] += core_in[p, l]
         pair[p] = send(part.at[p, 1 - yl, mine, :], pair_in.at[p], s_pair.at[p], r_pair.at[p], device(m=1))
 
+    def lanes(value):
+        return jnp.broadcast_to(value, (1, 128))
+
+    def weight_sums():
+        own_weights.start()
+        own_weights.wait()
+        for p in range(4):
+            total = jnp.zeros((8, 1024), jnp.float32)
+            for i in range(16):
+                block = share[p, 8 * i : 8 * i + 8, :]
+                total = total + block * block
+            sum1[row_slot, 2, p : p + 1, :] = lanes(jnp.sum(total))
+
+    def exact_dot(a, b, dims):
+        return lax.dot_general(
+            a, b, (dims, ((), ())), precision=lax.Precision.HIGHEST, preferred_element_type=jnp.float32
+        )
+
+    row_slot, col_slot = z * 2 + yh, x * 4 + yl * 2 + c
+
+    def statistics(p):
+        squares = final[p] * final[p] + 1e-30
+        colx[col_slot, p : p + 1, :] = jnp.sum(squares, axis=0, keepdims=True)
+        sums = exact_dot(jnp.ones((8, HALF), jnp.float32), squares, ((1,), (1,)))
+        rowx[row_slot, p : p + 1, :] = sums[0:1]
+
+    def exchange(buf, slot, peers, ss, rs):
+        return [send(buf.at[slot], buf.at[slot], ss.at[k], rs.at[k], to) for k, to in peers]
+
+    def landed(copies):
+        for copy in copies:
+            copy.wait_recv()
+
     def finish(p):
         pair[p].wait_recv()
         final[p] = part[p, yl, mine, :] + pair_in[p]
+        statistics(p)
+        if p == 3:
+            stats.append(exchange(rowx, row_slot, row_peers, s_rx, r_rx))
+            stats.append(exchange(colx, col_slot, col_peers, s_cx, r_cx))
         here = out.at[p, mine, columns(yh)]
         to_y[p] = send(final.at[p], here, s_gy.at[p], r_gy.at[p], device(m=2))
         to_core[p] = send(final.at[p], here, s_gc.at[p], r_gc.at[p], device(other=True))
@@ -166,6 +211,7 @@
         there = out.at[p, mine, columns(1 - yh)]
         fwd[p] = send(there, there, s_gf.at[p], r_gf.at[p], device(other=True))
 
+    stats = []
     send_ry(0)
     for m in (1, 3, 2):
         send_ly(0, m)
@@ -177,6 +223,7 @@
         send_ly(1, m)
     send_ry(2)
     send_ry(3)
+    weight_sums()
     send_xb(0)
     send_xa(1)
     for m in (1, 3, 2):
@@ -216,6 +263,48 @@
     finish(2)
     forward(1)
     finish(3)
+
+    decay = 1.0 - float(STEP) ** (-0.8)
+    landed(stats[0])
+    sums = rowx[0]
+    for k in range(1, 8):
+        sums = sums + rowx[k]
+    rows_new = decay * row_moment[:, mine] + (1.0 - decay) * (sums / D)
+    rown[c] = rows_new
+    to_rn = send(rown.at[c], rown.at[c], s_rn.at[0], r_rn.at[0], device(other=True))
+    landed(stats[1])
+    sums = colx[0]
+    for k in range(1, 16):
+        sums = sums + colx[k]
+    cols_new = decay * col_moment[:, columns(yh)] + (1.0 - decay) * (sums / D)
+    coln[yh] = cols_new
+    to_cn = send(coln.at[yh], coln.at[yh], s_cn.at[0], r_cn.at[0], device(m=2))
+    for p in range(4):
+        sum1[row_slot, 0, p : p + 1, :] = lanes(jnp.sum(rows_new[p : p + 1]) * 0.125)
+        by_row = jnp.broadcast_to(1.0 / rows_new[p : p + 1], (8, TOK))
+        by_col = exact_dot(by_row, final[p] * final[p], ((1,), (0,)))
+        sum1[row_slot, 1, p : p + 1, :] = lanes(jnp.sum(by_col[0:1] / cols_new[p : p + 1]))
+    landed(exchange(sum1, row_slot, row_peers, s_s1, r_s1))
+    sums = sum1[0]
+    for k in range(1, 8):
+        sums = sums + sum1[k]
+    sum2[col_slot] = sums
+    landed(exchange(sum2, col_slot, col_peers, s_s2, r_s2))
+    sums = sum2[0]
+    for k in range(1, 16):
+        sums = sums + sum2[k]
+    mean_row = sums[0] / D
+    clip = jnp.maximum(1.0, jnp.sqrt(sums[1] * mean_row / (D * D)))
+    size = min(0.01, float(STEP) ** (-0.5)) * jnp.maximum(0.001, jnp.sqrt(sums[2] / (D * D)))
+    factor = (-(size / clip) * jnp.sqrt(mean_row))[:, 0:1]
+    to_rn.wait_recv()
+    to_cn.wait_recv()
+    for k in range(2):
+        out_row[:, TOK * k : TOK * (k + 1)] = rown[k]
+        out_left[:, TOK * k : TOK * (k + 1)] = factor * lax.rsqrt(rown[k])
+        out_col[:, HALF * k : HALF * (k + 1)] = coln[k]
+        out_right[:, HALF * k : HALF * (k + 1)] = lax.rsqrt(coln[k])
+
     forward(2)
     forward(3)
     for p in range(4):
@@ -226,59 +315,55 @@
         copy.wait_send()
 
 
-def gradients(inputs, out_grads):
+def gradients(inputs, out_grads, weights, row_moment, col_moment):
     dma = pltpu.SemaphoreType.DMA
     any_space = pl.BlockSpec(memory_space=pl.ANY)
+    vmem = pl.BlockSpec(memory_space=pltpu.VMEM)
+    f32 = jnp.float32
     return pl.pallas_call(
         gradient_kernel,
-        out_shape=jax.ShapeDtypeStruct((4, 512, 1024), jnp.float32),
-        in_specs=[any_space, any_space],
-        out_specs=any_space,
+        out_shape=[
+            jax.ShapeDtypeStruct((4, 512, 1024), f32),
+            jax.ShapeDtypeStruct((4, 512), f32),
+            jax.ShapeDtypeStruct((4, 1024), f32),
+            jax.ShapeDtypeStruct((4, 512), f32),
+            jax.ShapeDtypeStruct((4, 1024), f32),
+        ],
+        in_specs=[any_space, any_space, any_space, vmem, vmem],
+        out_specs=[any_space, vmem, vmem, vmem, vmem],
         scratch_shapes=[
             pltpu.VMEM((2, 2, 4, 2, TOK, HALF), jnp.bfloat16),
             pltpu.VMEM((4, 4, 2, TOK, HALF), jnp.bfloat16),
-            pltpu.VMEM((4, 2, 512, HALF), jnp.float32),
-            pltpu.VMEM((4, 2, TOK, HALF), jnp.float32),
-            pltpu.VMEM((4, TOK, HALF), jnp.float32),
-            pltpu.VMEM((4, TOK, HALF), jnp.float32),
+            pltpu.VMEM((4, 2, 512, HALF), f32),
+            pltpu.VMEM((4, 2, TOK, HALF), f32),
+            pltpu.VMEM((4, TOK, HALF), f32),
+            pltpu.VMEM((4, TOK, HALF), f32),
+            pltpu.VMEM((4, 128, 1024), f32),
+            pltpu.VMEM((8, 4, TOK), f32),
+            pltpu.VMEM((16, 4, HALF), f32),
+            pltpu.VMEM((2, 4, TOK), f32),
+            pltpu.VMEM((2, 4, HALF), f32),
+            pltpu.VMEM((8, 3, 4, 128), f32),
+            pltpu.VMEM((16, 3, 4, 128), f32),
             dma((6,)),
             dma((2, 3)), dma((2, 3)), dma((4,)), dma((4,)),
             dma((4, 2)), dma((4, 2)), dma((4, 2)), dma((4, 2)), dma((4, 2)), dma((4, 2)),
             dma((2, 4, 2)), dma((2, 4, 2)), dma((2, 4)), dma((2, 4)),
             dma((4, 2)), dma((4, 2)), dma((4,)), dma((4,)),
             dma((4,)), dma((4,)), dma((4,)), dma((4,)), dma((4,)), dma((4,)), dma((4,)),
+            dma((1,)), dma((8,)), dma((8,)), dma((16,)), dma((16,)),
+            dma((1,)), dma((1,)), dma((1,)), dma((1,)), dma((8,)), dma((8,)), dma((16,)), dma((16,)),
         ],
         name="gradients",
         compiler_params=pltpu.CompilerParams(
             collective_id=0, has_side_effects=True, vmem_limit_bytes=56 * 2**20
         ),
-    )(inputs, out_grads)
+    )(inputs, out_grads, weights, row_moment, col_moment)
 
 
 def local(inputs, out_grads, weights, row_moment, col_moment):
-    decay_rate = 1.0 - float(STEP) ** (-0.8)
-    relative = min(0.01, float(STEP) ** (-0.5))
-    gradient = gradients(inputs, out_grads)
-    squares = gradient * gradient + 1e-30
-    row_part = jnp.sum(squares, 2)
-    col_part = jnp.sum(squares, 1)
-    param_part = jnp.sum(weights * weights, (1, 2))
-    row_sums = lax.psum(row_part, "col")
-    row_new = decay_rate * row_moment + (1.0 - decay_rate) * (row_sums / D)
-    col_sums = lax.psum(col_part, "row")
-    row_total = lax.psum(jnp.sum(row_new, 1), "row")
-    param_total = lax.psum(param_part, ("row", "col"))
-    col_new = decay_rate * col_moment + (1.0 - decay_rate) * (col_sums / D)
-    mean_row = row_total / D
-    update = gradient * lax.rsqrt(
-        row_new[:, :, None] * col_new[:, None, :] / mean_row[:, None, None]
-    )
-    update_part = jnp.sum(update * update, (1, 2))
-    update_total = lax.psum(update_part, ("row", "col"))
-    clip_factor = jnp.maximum(1.0, jnp.sqrt(update_total / (D * D)))
-    step_size = relative * jnp.maximum(0.001, jnp.sqrt(param_total / (D * D)))
-    change = -(step_size / clip_factor)[:, None, None] * update
-    return (change, row_new, col_new)
+    gradient, row_new, col_new, left, right = gradients(inputs, out_grads, weights, row_moment, col_moment)
+    return (gradient * (left[:, :, None] * right[:, None, :]), row_new, col_new)
 
 
 def solution(mesh):

time: 296 us -> 179 us (0.60)
  blocking collectives: 120 us -> 0 us
  Pallas kernels: 154 us -> 168 us
  other arithmetic: 20.2 us -> 7.62 us
    psum x3 -> x0, blocking collectives: 120 us -> none  [the longest x1 78.4 us: local(): update_total = lax.psum(update_part, ('row', 'col'))]
    reduce_sum x4 -> x0, other arithmetic: 13.8 us -> none  [the longest x1 4.8 us: local(): col_part = jnp.sum(squares, 1)]
    pallas_call x1, Pallas kernels: 154 us -> 168 us  [gradients(): pl.pallas_call(gradient_kernel, out_shape=[jax.ShapeDtypeStruct((4, 512,...]
where the time goes in v2:
time: 179 us; the launch traced here: 177 us
  Pallas kernels  168 us (94%)
  other arithmetic  7.62 us (4%)
    pallas_call x1, Pallas kernels, gradients(): pl.pallas_call(gradient_kernel, out_shape=[jax.ShapeDtypeStruct((4, 512,...  168 us
    mul x1, other arithmetic, local(): return (gradient * (left[:, :, None] * right[:, None, :]), row_new, col_new)  7.62 us

profile of v2, /device:TPU:0, one launch (start us, length us, event | category | flops | bytes accessed | tf_op | source)
XLA Modules:
  0.0 177.4 jit_solution(18167671400445990762)
XLA Ops:
  0.6 167.9 %gradients.1 = (f32[4,512,1024]{2,1,0:T(8,128)}, f32[4,512]{1,0:T(4,128)}, f32[4,1024]{1,0:T(4,128)}, f32[4,512]{1,0:T(4,128)}, f32[4,1024]{1,0:T(4,128)}) custom-call(bf16[2,512,512]{2,1,0:T(8,128)(2,1)} %inputs.1, bf16[4,256,1024]{2,1,0:T(8,128)(2,1)} %out_grads.1, f32[4,512,1024]{2,1,0:T(8,128)} %weights.1, f32[4,512]{1,0:T(4,128)} %row_moment.1, ...), custom_call_target="tpu_custom_call" | custom-call | tf_op jit(solution)/shard_map/gradients/pallas_call | solution.py:323
  168.5 0.0 copy-start.1
  168.5 0.0 copy-start
  168.6 7.6 %multiply_multiply_fusion = f32[4,512,1024]{2,1,0:T(8,128)} fusion(f32[4,512,1024]{2,1,0:T(8,128)} %get-tuple-element.8, f32[4,1024]{1,0:T(4,128)} %get-tuple-element.10, f32[4,512]{1,0:T(4,128)} %get-tuple-element.9), kind=kLoop, calls=%fused_computation | loop fusion | flops 4194304 | bytes 16801792 | tf_op jit(solution)/shard_map/mul | solution.py:366
  176.2 0.0 copy-done.1
  176.2 0.6 copy.10
  176.8 0.0 copy-done
  176.8 0.6 copy.11
Async XLA Ops:
  168.5 7.6 %copy-start.1 = (f32[4,512]{1,0:T(4,128)S(1)}, f32[4,512]{1,0:T(4,128)}, u32[]{:S(2)}) copy-start(f32[4,512]{1,0:T(4,128)} %get-tuple-element.17) | copy-start | bytes 24580
  168.5 8.2 %copy-start = (f32[4,1024]{1,0:T(4,128)S(1)}, f32[4,1024]{1,0:T(4,128)}, u32[]{:S(2)}) copy-start(f32[4,1024]{1,0:T(4,128)} %get-tuple-element.18) | copy-start | bytes 49156

commit v3 on v2

--- a/solution.py
+++ b/solution.py
@@ -12,9 +12,30 @@
 HALF = 512
 
 
+TOP = 2.0**7.75
+
+
+def encode(v):
+    square = v * v
+    fourth = square * square
+    eighth = fourth * fourth
+    power = eighth * eighth
+    return jnp.where(v < 0, -power, power)
+
+
+def decode(y):
+    root = lax.rsqrt(lax.rsqrt(lax.rsqrt(lax.rsqrt(jnp.abs(y)))))
+    return jnp.where(y == 0, 0.0, jnp.where(y < 0, -root, root))
+
+
+def scale_kernel(code, left, right, out):
+    col = jnp.transpose(left[0, 0])[:, 0:1]
+    out[0] = decode(code[0].astype(jnp.float32)) * col * right[0]
+
+
 def gradient_kernel(
     inputs, out_grads, weights, row_moment, col_moment, out, out_row, out_col, out_left, out_right,
-    lbuf, rbuf, part, core_in, pair_in, final, share, rowx, colx, rown, coln, sum1, sum2,
+    lbuf, rbuf, part, core_in, pair_in, final, code, share, rowx, colx, rown, coln, sum1, sum2,
     s_loc, s_ly, r_ly, s_ry, r_ry, s_xa, r_xa, s_xb, r_xb, s_xf, r_xf,
     s_z, r_z, s_zf, r_zf, s_core, r_core, s_pair, r_pair, s_gc, r_gc, s_gy, r_gy, s_gf, r_gf, s_out,
     s_share, s_rx, r_rx, s_cx, r_cx, s_rn, r_rn, s_cn, r_cn, s_s1, r_s1, s_s2, r_s2,
@@ -194,15 +215,18 @@
 
     def finish(p):
         pair[p].wait_recv()
-        final[p] = part[p, yl, mine, :] + pair_in[p]
+        gradient = part[p, yl, mine, :] + pair_in[p]
+        final[p] = gradient
         statistics(p)
         if p == 3:
             stats.append(exchange(rowx, row_slot, row_peers, s_rx, r_rx))
             stats.append(exchange(colx, col_slot, col_peers, s_cx, r_cx))
+        norm = jnp.sum(gradient * gradient + 1e-30, axis=1, keepdims=True)
+        code[p] = encode(gradient * (TOP * lax.rsqrt(norm))).astype(jnp.bfloat16)
         here = out.at[p, mine, columns(yh)]
-        to_y[p] = send(final.at[p], here, s_gy.at[p], r_gy.at[p], device(m=2))
-        to_core[p] = send(final.at[p], here, s_gc.at[p], r_gc.at[p], device(other=True))
-        copy = pltpu.make_async_copy(final.at[p], here, s_out.at[p])
+        to_y[p] = send(code.at[p], here, s_gy.at[p], r_gy.at[p], device(m=2))
+        to_core[p] = send(code.at[p], here, s_gc.at[p], r_gc.at[p], device(other=True))
+        copy = pltpu.make_async_copy(code.at[p], here, s_out.at[p])
         copy.start()
         outs.append(copy)
 
@@ -270,7 +294,9 @@
     for k in range(1, 8):
         sums = sums + rowx[k]
     rows_new = decay * row_moment[:, mine] + (1.0 - decay) * (sums / D)
-    rown[c] = rows_new
+    rown[c, 0] = rows_new
+    for h in range(2):
+        rown[c, 1 + h] = rowx[z * 2 + h]
     to_rn = send(rown.at[c], rown.at[c], s_rn.at[0], r_rn.at[0], device(other=True))
     landed(stats[1])
     sums = colx[0]
@@ -300,10 +326,15 @@
     to_rn.wait_recv()
     to_cn.wait_recv()
     for k in range(2):
-        out_row[:, TOK * k : TOK * (k + 1)] = rown[k]
-        out_left[:, TOK * k : TOK * (k + 1)] = factor * lax.rsqrt(rown[k])
+        out_row[:, TOK * k : TOK * (k + 1)] = rown[k, 0]
+        for h in range(2):
+            rows_left = factor * lax.rsqrt(rown[k, 0]) * jnp.sqrt(rown[k, 1 + h]) * (1.0 / TOP)
+            for p in range(4):
+                out_left[p, h, :, TOK * k : TOK * (k + 1)] = jnp.broadcast_to(rows_left[p : p + 1], (8, TOK))
         out_col[:, HALF * k : HALF * (k + 1)] = coln[k]
-        out_right[:, HALF * k : HALF * (k + 1)] = lax.rsqrt(coln[k])
+        cols_right = lax.rsqrt(coln[k])
+        for p in range(4):
+            out_right[p, :, HALF * k : HALF * (k + 1)] = cols_right[p : p + 1]
 
     forward(2)
     forward(3)
@@ -323,11 +354,11 @@
     return pl.pallas_call(
         gradient_kernel,
         out_shape=[
-            jax.ShapeDtypeStruct((4, 512, 1024), f32),
+            jax.ShapeDtypeStruct((4, 512, 1024), jnp.bfloat16),
             jax.ShapeDtypeStruct((4, 512), f32),
             jax.ShapeDtypeStruct((4, 1024), f32),
-            jax.ShapeDtypeStruct((4, 512), f32),
-            jax.ShapeDtypeStruct((4, 1024), f32),
+            jax.ShapeDtypeStruct((4, 2, 8, 512), f32),
+            jax.ShapeDtypeStruct((4, 1, 1024), f32),
         ],
         in_specs=[any_space, any_space, any_space, vmem, vmem],
         out_specs=[any_space, vmem, vmem, vmem, vmem],
@@ -338,10 +369,11 @@
             pltpu.VMEM((4, 2, TOK, HALF), f32),
             pltpu.VMEM((4, TOK, HALF), f32),
             pltpu.VMEM((4, TOK, HALF), f32),
+            pltpu.VMEM((4, TOK, HALF), jnp.bfloat16),
             pltpu.VMEM((4, 128, 1024), f32),
             pltpu.VMEM((8, 4, TOK), f32),
             pltpu.VMEM((16, 4, HALF), f32),
-            pltpu.VMEM((2, 4, TOK), f32),
+            pltpu.VMEM((2, 3, 4, TOK), f32),
             pltpu.VMEM((2, 4, HALF), f32),
             pltpu.VMEM((8, 3, 4, 128), f32),
             pltpu.VMEM((16, 3, 4, 128), f32),
@@ -362,8 +394,20 @@
 
 
 def local(inputs, out_grads, weights, row_moment, col_moment):
-    gradient, row_new, col_new, left, right = gradients(inputs, out_grads, weights, row_moment, col_moment)
-    return (gradient * (left[:, :, None] * right[:, None, :]), row_new, col_new)
+    code, row_new, col_new, left, right = gradients(inputs, out_grads, weights, row_moment, col_moment)
+    change = pl.pallas_call(
+        scale_kernel,
+        out_shape=jax.ShapeDtypeStruct((4, 512, 1024), jnp.float32),
+        grid=(4, 2),
+        in_specs=[
+            pl.BlockSpec((1, 512, HALF), lambda p, h: (p, 0, h)),
+            pl.BlockSpec((1, 1, 8, 512), lambda p, h: (p, h, 0, 0)),
+            pl.BlockSpec((1, 1, HALF), lambda p, h: (p, 0, h)),
+        ],
+        out_specs=pl.BlockSpec((1, 512, HALF), lambda p, h: (p, 0, h)),
+        name="scale",
+    )(code, left, right)
+    return (change, row_new, col_new)
 
 
 def solution(mesh):

time: 179 us -> 158 us (0.88)
  Pallas kernels: 168 us -> 155 us
  other arithmetic: 7.62 us -> 0 us
    pallas_call x1, Pallas kernels: 168 us -> 145 us  [gradients(): pl.pallas_call(gradient_kernel, out_shape=[jax.ShapeDtypeStruct((4, 512,...]
    pallas_call x0 -> x1, Pallas kernels: none -> 9.76 us  [local(): pl.pallas_call(scale_kernel, out_shape=jax.ShapeDtypeStruct((4, 512, 1024...]
    mul x1 -> x0, other arithmetic: 7.62 us -> none  [local(): return (gradient * (left[:, :, None] * right[:, None, :]), row_new, col_new)]
where the time goes in v3:
time: 158 us; the launch traced here: 157 us
  Pallas kernels  155 us (98%)
    pallas_call x1, Pallas kernels, gradients(): pl.pallas_call(gradient_kernel, out_shape=[jax.ShapeDtypeStruct((4, 512,...  145 us
    pallas_call x1, Pallas kernels, local(): pl.pallas_call(scale_kernel, out_shape=jax.ShapeDtypeStruct((4, 512, 1024...  9.76 us

profile of v3, /device:TPU:0, one launch (start us, length us, event | category | flops | bytes accessed | tf_op | source)
XLA Modules:
  0.0 156.6 jit_solution(14753858246714651272)
XLA Ops:
  0.6 145.0 %gradients.1 = (bf16[4,512,1024]{2,1,0:T(8,128)(2,1)}, f32[4,512]{1,0:T(4,128)}, f32[4,1024]{1,0:T(4,128)}, f32[4,2,8,512]{3,2,1,0:T(8,128)}, f32[4,1,1024]{2,1,0:T(1,128)}) custom-call(bf16[2,512,512]{2,1,0:T(8,128)(2,1)} %inputs.1, bf16[4,256,1024]{2,1,0:T(8,128)(2,1)} %out_grads.1, f32[4,512,1024]{2,1,0:T(8,128)} %weights.1, f32[4,512]{1,0:T(4,128)} %row_moment.1, ...), custom_call_target="tpu_custom_call" | custom-call | tf_op jit(solution)/shard_map/gradients/pallas_call | solution.py:354
  145.6 0.0 copy-start.1
  145.6 0.0 copy-start
  145.6 9.8 %scale.1 = f32[4,512,1024]{2,1,0:T(8,128)} custom-call(bf16[4,512,1024]{2,1,0:T(8,128)(2,1)} %get-tuple-element.8.code, f32[4,2,8,512]{3,2,1,0:T(8,128)} %get-tuple-element.9.left, f32[4,1,1024]{2,1,0:T(1,128)} %get-tuple-element.10.right), custom_call_target="tpu_custom_call" | custom-call | tf_op jit(solution)/shard_map/scale/pallas_call | solution.py:398
  155.4 0.0 copy-done.1
  155.4 0.6 copy.10
  156.0 0.0 copy-done
  156.0 0.6 copy.11
Async XLA Ops:
  145.6 9.8 %copy-start.1 = (f32[4,512]{1,0:T(4,128)S(1)}, f32[4,512]{1,0:T(4,128)}, u32[]{:S(2)}) copy-start(f32[4,512]{1,0:T(4,128)} %get-tuple-element.17) | copy-start | bytes 24580
  145.6 10.4 %copy-start = (f32[4,1024]{1,0:T(4,128)S(1)}, f32[4,1024]{1,0:T(4,128)}, u32[]{:S(2)}) copy-start(f32[4,1024]{1,0:T(4,128)} %get-tuple-element.18) | copy-start | bytes 49156

commit v4 on v3

v4 whole, which is shorter than its diff:
```python
import jax
import jax.numpy as jnp
from jax import lax
from jax.experimental import pallas as pl
from jax.experimental.pallas import tpu as pltpu
from jax.sharding import PartitionSpec as P

D = 4096
STEP = 10
MESH = pl.DeviceIdType.MESH
TOK = 256
HALF = 512


TOP = 2.0**7.75


def encode(v):
    square = v * v
    fourth = square * square
    eighth = fourth * fourth
    power = eighth * eighth
    return jnp.where(v < 0, -power, power)


def decode(y):
    return y * jnp.exp2(jnp.log2(jnp.maximum(jnp.abs(y), 1e-37)) * (-15.0 / 16.0))


def scale_kernel(
    code, left_in, right_in, row_new, col_new, out, out_row, out_col, codes, changes, left, right, s_in, s_out, s_small
):
    blocks = [(p, i) for p in range(4) for i in range(2)]
    rows = [pl.ds(TOK * i, TOK) for i in range(2)]
    loads = [pltpu.make_async_copy(code.at[p, rows[i]], codes.at[p, rows[i]], s_in.at[p, i]) for p, i in blocks]
    stores = [pltpu.make_async_copy(changes.at[p, rows[i]], out.at[p, rows[i]], s_out.at[p, i]) for p, i in blocks]
    small = [
        pltpu.make_async_copy(a, b, s_small.at[k])
        for k, (a, b) in enumerate([(left_in, left), (right_in, right), (row_new, out_row), (col_new, out_col)])
    ]
    for load in small + loads:
        load.start()
    small[0].wait()
    small[1].wait()
    for k, (p, i) in enumerate(blocks):
        loads[k].wait()
        for h in range(2):
            cols = pl.ds(HALF * h, HALF)
            col = jnp.transpose(left[p, h, :, rows[i]])[:, 0:1]
            changes[p, rows[i], cols] = decode(codes[p, rows[i], cols].astype(jnp.float32)) * (col * right[p, :, cols])
        stores[k].start()
    for store in stores + small[2:]:
        store.wait()


def gradient_kernel(
    inputs, out_grads, weights, row_moment, col_moment, out, out_row, out_col, out_left, out_right,
    lbuf, rbuf, part, core_in, pair_in, final, code, share, rowx, colx, dcolx, rown, coln, sum1, sum2,
    s_loc, s_ly, r_ly, s_ry, r_ry, s_xa, r_xa, s_xb, r_xb, s_xf, r_xf,
    s_z, r_z, s_zf, r_zf, s_core, r_core, s_pair, r_pair, s_gc, r_gc, s_gy, r_gy, s_gf, r_gf, s_out,
    s_share, s_rx, r_rx, s_cx, r_cx, s_dx, r_dx, s_rn, r_rn, s_cn, r_cn, s_s1, r_s1, s_s2, r_s2,
):
    dp, row, z = lax.axis_index("dp"), lax.axis_index("row"), lax.axis_index("col")
    yh, c, x, yl = dp // 2, dp % 2, row // 2, row % 2

    def device(dx=0, m=0, dz=0, other=False):
        h = 1 - yh if m & 2 else yh
        l = 1 - yl if m & 1 else yl
        return {
            "dp": h * 2 + (1 - c if other else c),
            "row": ((x + dx) % 4) * 2 + l,
            "col": (z + dz) % 4,
        }

    def send(src, dst, ss, rs, to):
        copy = pltpu.make_async_remote_copy(
            src_ref=src, dst_ref=dst, send_sem=ss, recv_sem=rs, device_id=to, device_id_type=MESH
        )
        copy.start()
        sent.append(copy)
        return copy

    sent, drained = [], [0]

    def drain(count):
        for copy in sent[drained[0] : count]:
            copy.wait_send()
        drained[0] = max(drained[0], count)

    half = [yh, (yh + yl) % 2, yh, (yh + yl) % 2]
    row_peers = [(dz * 2 + h, device(dz=dz, m=2 * h)) for dz in range(4) for h in range(2) if dz + h]
    col_peers = [
        (dx * 4 + l * 2 + o, device(dx=dx, m=l, other=bool(o)))
        for dx in range(4) for l in range(2) for o in range(2) if dx + l + o
    ]
    diagonal_peers = [
        (dx * 4 + l * 2 + o, device(dx=dx, m=3 * l, other=bool(o)))
        for dx in range(4) for l in range(2) for o in range(2) if dx + l + o
    ]
    plane_peers = [(dx * 4 + dz, device(dx=dx, dz=dz)) for dx in range(4) for dz in range(4) if dx + dz]
    line_peers = [(m * 2 + o, device(m=m, other=bool(o))) for m in range(4) for o in range(2) if m + o]
    neighbours = [to for _, to in row_peers + col_peers] + [to for k, to in diagonal_peers if k & 2]
    neighbours += [to for k, to in plane_peers if k // 4 and k % 4] + [to for k, to in line_peers if k == 5]
    barrier = pltpu.get_barrier_semaphore()
    for other in neighbours:
        pl.semaphore_signal(barrier, inc=1, device_id=other, device_id_type=MESH)
    pl.semaphore_wait(barrier, len(neighbours))

    def flip(bit, value):
        return 1 - value if bit else value

    def columns(h):
        return pl.ds(pl.multiple_of(h * HALF, HALF), HALF)

    def l_part(s, m, dz=0):
        return lbuf.at[s, flip(m & 1, yl), (z + dz) % 4, flip(m & 2, yh)]

    def r_part(p, m, dx=0):
        return rbuf.at[p, (x + dx) % 4, flip(m, yh)]

    def own_tokens(h):
        return pl.ds(pl.multiple_of(h * TOK, TOK), TOK)

    quarter = pl.ds(pl.multiple_of(dp * 128, 128), 128)
    own_weights = pltpu.make_async_copy(weights.at[:, quarter, :], share, s_share.at[0])
    local = []
    for s in range(2):
        copy = pltpu.make_async_copy(inputs.at[s, own_tokens(yl), :], l_part(s, 0), s_loc.at[s])
        copy.start()
        local.append(copy)
    for p in range(4):
        copy = pltpu.make_async_copy(out_grads.at[p, :, columns(half[p])], r_part(p, 0), s_loc.at[2 + p])
        copy.start()
        local.append(copy)

    ly, ry, xa, xb, xf, zz, zf = {}, {}, {}, {}, {}, {}, {}

    def send_ly(s, m):
        rows = own_tokens(flip(m & 1, yl))
        ly[s, m] = send(inputs.at[s, rows, :], l_part(s, 0), s_ly.at[s, m - 1], r_ly.at[s, m - 1], device(m=m))

    def send_ry(p):
        ry[p] = send(out_grads.at[p, :, columns(1 - half[p])], r_part(p, 0), s_ry.at[p], r_ry.at[p], device(m=2))

    def send_xa(p, ways=(0, 1)):
        for d in ways:
            xa[p, d] = send(out_grads.at[p, :, columns(half[p])], r_part(p, 0), s_xa.at[p, d], r_xa.at[p, d], device(dx=1 - 2 * d))

    def send_xb(p, ways=(0, 1)):
        if not [k for k in xb if k[0] == p]:
            ry[p].wait_recv()
        for d in ways:
            xb[p, d] = send(r_part(p, 1), r_part(p, 1), s_xb.at[p, d], r_xb.at[p, d], device(dx=1 - 2 * d))

    def send_xfa(p):
        xa[p, 0].wait_recv()
        xf[p, 0] = send(r_part(p, 0, -1), r_part(p, 0, -1), s_xf.at[p, 0], r_xf.at[p, 0], device(dx=1))

    def send_xfb(p):
        xb[p, 1].wait_recv()
        xf[p, 1] = send(r_part(p, 1, 1), r_part(p, 1, 1), s_xf.at[p, 1], r_xf.at[p, 1], device(dx=-1))

    def send_z(s, m):
        if m:
            ly[s, m].wait_recv()
        for d in range(2):
            src = l_part(s, m) if m else inputs.at[s, own_tokens(yl), :]
            zz[s, m, d] = send(src, l_part(s, m), s_z.at[s, m, d], r_z.at[s, m, d], device(dz=1 - 2 * d))

    def send_zf(s, m):
        d = m // 2
        back = 2 * d - 1
        zz[s, m, d].wait_recv()
        zf[s, m] = send(l_part(s, m, back), l_part(s, m, back), s_zf.at[s, m], r_zf.at[s, m], device(dz=-back))

    core, pair, to_core, to_y, fwd, outs = {}, {}, {}, {}, {}, []
    mine = pl.ds(pl.multiple_of(c * TOK, TOK), TOK)
    theirs = pl.ds(pl.multiple_of((1 - c) * TOK, TOK), TOK)

    def wait_r(p):
        local[2 + p].wait()
        for d in range(2):
            if d == 1:
                xa[p, d].wait_recv()
            else:
                xb[p, d].wait_recv()
            xf[p, d].wait_recv()

    def wait_l(s):
        local[s].wait()
        for m in range(4):
            zz[s, m, 1 - m // 2].wait_recv()
            zf[s, m].wait_recv()

    def compute(p):
        s = 0 if p < 3 else 1
        right = rbuf[p].reshape(8 * TOK, HALF)

        def rows(l, rs):
            left = lbuf[s, l, :, :, :, rs].reshape(8 * TOK, TOK)
            part[p, l, rs, :] = lax.dot_general(
                left, right, (((0,), (0,)), ((), ())), preferred_element_type=jnp.float32
            )

        to = device(m=3 if p % 2 else 1)
        for k, l in enumerate((1 - yl, yl)):
            rows(l, theirs)
            core[p, k] = send(
                part.at[p, l, theirs, :], core_in.at[p, l], s_core.at[p, k], r_core.at[p, k], device(other=True)
            )
            rows(l, mine)
            core[p, k].wait_recv()
            part[p, l, mine, :] += core_in[p, l]
            if k == 0:
                pair[p] = send(part.at[p, l, mine, :], pair_in.at[p], s_pair.at[p], r_pair.at[p], to)

    def lanes(value):
        return jnp.broadcast_to(value, (1, 128))

    def weight_sums():
        own_weights.wait()
        for p in range(4):
            total = jnp.zeros((8, 1024), jnp.float32)
            for i in range(16):
                block = share[p, 8 * i : 8 * i + 8, :]
                total = total + block * block
            sum1[plane_slot, 2, p : p + 1, :] = lanes(jnp.sum(total))

    def exact_dot(a, b, dims):
        return lax.dot_general(
            a, b, (dims, ((), ())), precision=lax.Precision.HIGHEST, preferred_element_type=jnp.float32
        )

    plane_slot, line_slot = x * 4 + z, dp * 2 + yl
    row_slot, col_slot, dcol_slot = z * 2 + yh, x * 4 + yl * 2 + c, x * 4 + yh * 2 + c

    def statistics(p):
        squares = final[p] * final[p] + 1e-30
        sums = jnp.sum(squares, axis=0, keepdims=True)
        if p % 2:
            dcolx[dcol_slot, p // 2 : p // 2 + 1, :] = sums
        else:
            colx[col_slot, p // 2 : p // 2 + 1, :] = sums
        sums = exact_dot(jnp.ones((8, HALF), jnp.float32), squares, ((1,), (1,)))
        rowx[row_slot, p : p + 1, :] = sums[0:1]

    def exchange(buf, slot, peers, ss, rs):
        return [send(buf.at[slot], buf.at[slot], ss.at[k], rs.at[k], to) for k, to in peers]

    def landed(copies):
        for copy in copies:
            copy.wait_recv()

    def hand_on(p):
        here = out.at[p, mine, columns(half[p])]
        to_y[p] = send(code.at[p], here, s_gy.at[p], r_gy.at[p], device(m=2))
        to_core[p] = send(code.at[p], here, s_gc.at[p], r_gc.at[p], device(other=True))
        copy = pltpu.make_async_copy(code.at[p], here, s_out.at[p])
        copy.start()
        outs.append(copy)

    def finish(p):
        pair[p].wait_recv()
        gradient = part[p, yl, mine, :] + pair_in[p]
        final[p] = gradient
        statistics(p)
        if p == 2:
            stats.append(exchange(colx, col_slot, col_peers, s_cx, r_cx))
        if p == 3:
            stats.append(exchange(rowx, row_slot, row_peers, s_rx, r_rx))
            stats.append(exchange(dcolx, dcol_slot, diagonal_peers, s_dx, r_dx))
        norm = jnp.sum(gradient * gradient + 1e-30, axis=1, keepdims=True)
        code[p] = encode(gradient * (TOP * lax.rsqrt(norm))).astype(jnp.bfloat16)

    def forward(p):
        to_y[p].wait_recv()
        there = out.at[p, mine, columns(1 - half[p])]
        fwd[p] = send(there, there, s_gf.at[p], r_gf.at[p], device(other=True))

    stats = []
    send_ly(0, 1)
    send_ly(0, 3)
    send_xa(0)
    send_z(0, 0)
    send_xa(1)
    own_weights.start()
    send_z(0, 1)
    send_z(0, 3)
    send_ry(0)
    send_ly(0, 2)
    send_ry(1)
    send_xa(2)
    weight_sums()
    send_xb(0)
    send_xfa(0)
    send_z(0, 2)
    send_zf(0, 0)
    send_zf(0, 1)
    send_xfb(0)
    send_ry(2)
    send_xb(1)
    send_zf(0, 3)
    send_zf(0, 2)
    send_xfa(1)
    send_ly(1, 1)
    send_ly(1, 3)
    send_ly(1, 2)
    send_ry(3)
    send_z(1, 0)
    send_xfb(1)
    send_xb(2)
    send_xa(3, (0,))
    send_z(1, 1)
    early = len(sent) - 12
    wait_r(0)
    wait_l(0)
    compute(0)
    send_z(1, 3)
    send_xb(3, (1,))
    send_xfa(2)
    wait_r(1)
    compute(1)
    send_z(1, 2)
    send_xfb(2)
    send_xa(3, (1,))
    send_xb(3, (0,))
    send_zf(1, 0)
    send_zf(1, 1)
    send_zf(1, 3)
    drain(early // 2)
    finish(0)
    hand_on(0)
    send_zf(1, 2)
    send_xfa(3)
    send_xfb(3)
    drain(early)
    finish(1)
    hand_on(1)
    wait_r(2)
    late = len(sent) - 6
    compute(2)
    wait_r(3)
    wait_l(1)
    compute(3)
    drain(late)
    forward(0)
    finish(2)
    finish(3)
    hand_on(2)
    hand_on(3)

    decay = 1.0 - float(STEP) ** (-0.8)
    tail = len(sent)
    landed(stats[1])
    sums = rowx[0]
    for k in range(1, 8):
        sums = sums + rowx[k]
    rows_new = decay * row_moment[:, mine] + (1.0 - decay) * (sums / D)
    rown[c, 0] = rows_new
    for h in range(2):
        rown[c, 1 + h] = rowx[z * 2 + h]
    to_rn = send(rown.at[c], rown.at[c], s_rn.at[0], r_rn.at[0], device(other=True))
    landed(stats[0])
    sums = colx[0]
    for k in range(1, 16):
        sums = sums + colx[k]
    for p in (0, 2):
        old = col_moment[p : p + 1, columns(half[p])]
        coln[yh, p : p + 1, :] = decay * old + (1.0 - decay) * (sums[p // 2 : p // 2 + 1] / D)
    landed(stats[2])
    sums = dcolx[0]
    for k in range(1, 16):
        sums = sums + dcolx[k]
    for p in (1, 3):
        old = col_moment[p : p + 1, columns(half[p])]
        coln[yh, p : p + 1, :] = decay * old + (1.0 - decay) * (sums[p // 2 : p // 2 + 1] / D)
    cols_new = coln[yh]
    to_cn = send(coln.at[yh], coln.at[yh], s_cn.at[0], r_cn.at[0], device(m=2))
    for p in range(4):
        sum1[plane_slot, 0, p : p + 1, :] = lanes(jnp.sum(rows_new[p : p + 1]) * 0.125)
        by_row = jnp.broadcast_to(1.0 / rows_new[p : p + 1], (8, TOK))
        by_col = exact_dot(by_row, final[p] * final[p], ((1,), (0,)))
        sum1[plane_slot, 1, p : p + 1, :] = lanes(jnp.sum(by_col[0:1] / cols_new[p : p + 1]))
    landed(exchange(sum1, plane_slot, plane_peers, s_s1, r_s1))
    sums = sum1[0]
    for k in range(1, 16):
        sums = sums + sum1[k]
    sum2[line_slot] = sums
    lines = exchange(sum2, line_slot, line_peers, s_s2, r_s2)
    drain(tail)
    forward(1)
    forward(2)
    forward(3)
    landed(lines)
    sums = sum2[0]
    for k in range(1, 8):
        sums = sums + sum2[k]
    mean_row = sums[0] / D
    clip = jnp.maximum(1.0, jnp.sqrt(sums[1] * mean_row / (D * D)))
    size = min(0.01, float(STEP) ** (-0.5)) * jnp.maximum(0.001, jnp.sqrt(sums[2] / (D * D)))
    factor = (-(size / clip) * jnp.sqrt(mean_row))[:, 0:1]
    to_rn.wait_recv()
    to_cn.wait_recv()
    for k in range(2):
        out_row[:, TOK * k : TOK * (k + 1)] = rown[k, 0]
        for h in range(2):
            rows_left = factor * lax.rsqrt(rown[k, 0]) * jnp.sqrt(rown[k, 1 + h]) * (1.0 / TOP)
            for p in range(4):
                out_left[p, (h + yl) % 2 if p % 2 else h, :, TOK * k : TOK * (k + 1)] = jnp.broadcast_to(rows_left[p : p + 1], (8, TOK))
        cols_right = lax.rsqrt(coln[k])
        for p in range(4):
            place = columns((k + yl) % 2) if p % 2 else pl.ds(HALF * k, HALF)
            out_col[p : p + 1, place] = coln[k, p : p + 1, :]
            out_right[p, :, place] = cols_right[p : p + 1]

    for p in range(4):
        to_core[p].wait_recv()
        fwd[p].wait_recv()
        outs[p].wait()
    drain(len(sent))


def gradients(inputs, out_grads, weights, row_moment, col_moment):
    dma = pltpu.SemaphoreType.DMA
    any_space = pl.BlockSpec(memory_space=pl.ANY)
    vmem = pl.BlockSpec(memory_space=pltpu.VMEM)
    f32 = jnp.float32
    return pl.pallas_call(
        gradient_kernel,
        out_shape=[
            jax.ShapeDtypeStruct((4, 512, 1024), jnp.bfloat16),
            jax.ShapeDtypeStruct((4, 512), f32),
            jax.ShapeDtypeStruct((4, 1024), f32),
            jax.ShapeDtypeStruct((4, 2, 8, 512), f32),
            jax.ShapeDtypeStruct((4, 1, 1024), f32),
        ],
        in_specs=[any_space, any_space, any_space, vmem, vmem],
        out_specs=[any_space, vmem, vmem, vmem, vmem],
        scratch_shapes=[
            pltpu.VMEM((2, 2, 4, 2, TOK, HALF), jnp.bfloat16),
            pltpu.VMEM((4, 4, 2, TOK, HALF), jnp.bfloat16),
            pltpu.VMEM((4, 2, 512, HALF), f32),
            pltpu.VMEM((4, 2, TOK, HALF), f32),
            pltpu.VMEM((4, TOK, HALF), f32),
            pltpu.VMEM((4, TOK, HALF), f32),
            pltpu.VMEM((4, TOK, HALF), jnp.bfloat16),
            pltpu.VMEM((4, 128, 1024), f32),
            pltpu.VMEM((8, 4, TOK), f32),
            pltpu.VMEM((16, 2, HALF), f32),
            pltpu.VMEM((16, 2, HALF), f32),
            pltpu.VMEM((2, 3, 4, TOK), f32),
            pltpu.VMEM((2, 4, HALF), f32),
            pltpu.VMEM((16, 3, 4, 128), f32),
            pltpu.VMEM((8, 3, 4, 128), f32),
            dma((6,)),
            dma((2, 3)), dma((2, 3)), dma((4,)), dma((4,)),
            dma((4, 2)), dma((4, 2)), dma((4, 2)), dma((4, 2)), dma((4, 2)), dma((4, 2)),
            dma((2, 4, 2)), dma((2, 4, 2)), dma((2, 4)), dma((2, 4)),
            dma((4, 2)), dma((4, 2)), dma((4,)), dma((4,)),
            dma((4,)), dma((4,)), dma((4,)), dma((4,)), dma((4,)), dma((4,)), dma((4,)),
            dma((1,)), dma((8,)), dma((8,)), dma((16,)), dma((16,)), dma((16,)), dma((16,)),
            dma((1,)), dma((1,)), dma((1,)), dma((1,)), dma((16,)), dma((16,)), dma((8,)), dma((8,)),
        ],
        name="gradients",
        compiler_params=pltpu.CompilerParams(
            collective_id=0, has_side_effects=True, vmem_limit_bytes=56 * 2**20
        ),
    )(inputs, out_grads, weights, row_moment, col_moment)


def local(inputs, out_grads, weights, row_moment, col_moment):
    code, row_new, col_new, left, right = gradients(inputs, out_grads, weights, row_moment, col_moment)
    any_space = pl.BlockSpec(memory_space=pl.ANY)
    f32 = jnp.float32
    return pl.pallas_call(
        scale_kernel,
        out_shape=[
            jax.ShapeDtypeStruct((4, 512, 1024), f32),
            jax.ShapeDtypeStruct((4, 512), f32),
            jax.ShapeDtypeStruct((4, 1024), f32),
        ],
        in_specs=[any_space] * 5,
        out_specs=[any_space] * 3,
        scratch_shapes=[
            pltpu.VMEM((4, 512, 1024), jnp.bfloat16),
            pltpu.VMEM((4, 512, 1024), f32),
            pltpu.VMEM((4, 2, 8, 512), f32),
            pltpu.VMEM((4, 1, 1024), f32),
            pltpu.SemaphoreType.DMA((4, 2)),
            pltpu.SemaphoreType.DMA((4, 2)),
            pltpu.SemaphoreType.DMA((4,)),
        ],
        name="scale",
        compiler_params=pltpu.CompilerParams(vmem_limit_bytes=60 * 2**20),
    )(code, left, right, row_new, col_new)


def solution(mesh):
    return jax.shard_map(
        local,
        mesh=mesh,
        in_specs=(
            P(None, ("dp", "col"), "row"),
            P(None, ("dp", "row"), "col"),
            P(None, "row", "col"),
            P(None, "row"),
            P(None, "col"),
        ),
        out_specs=(P(None, "row", "col"), P(None, "row"), P(None, "col")),
        check_vma=False,
    )
```

time: 158 us -> 139 us (0.88)
  Pallas kernels: 155 us -> 137 us
    pallas_call x1, Pallas kernels: 145 us -> 131 us  [gradients(): pl.pallas_call(gradient_kernel, out_shape=[jax.ShapeDtypeStruct((4, 512,...]
    pallas_call x1, Pallas kernels: 9.76 us -> 5.62 us  [local(): pl.pallas_call(scale_kernel, out_shape=[jax.ShapeDtypeStruct((4, 512, 102...]
where the time goes in v4:
time: 139 us; the launch traced here: 137 us
  Pallas kernels  137 us (99%)
    pallas_call x1, Pallas kernels, gradients(): pl.pallas_call(gradient_kernel, out_shape=[jax.ShapeDtypeStruct((4, 512,...  131 us
    pallas_call x1, Pallas kernels, local(): pl.pallas_call(scale_kernel, out_shape=[jax.ShapeDtypeStruct((4, 512, 102...  5.62 us

profile of v4, /device:TPU:0, one launch (start us, length us, event | category | flops | bytes accessed | tf_op | source)
XLA Modules:
  0.0 137.3 jit_solution(5209963398998766187)
XLA Ops:
  0.6 130.9 %gradients.1 = (bf16[4,512,1024]{2,1,0:T(8,128)(2,1)}, f32[4,512]{1,0:T(4,128)}, f32[4,1024]{1,0:T(4,128)}, f32[4,2,8,512]{3,2,1,0:T(8,128)}, f32[4,1,1024]{2,1,0:T(1,128)}) custom-call(bf16[2,512,512]{2,1,0:T(8,128)(2,1)} %inputs.1, bf16[4,256,1024]{2,1,0:T(8,128)(2,1)} %out_grads.1, f32[4,512,1024]{2,1,0:T(8,128)} %weights.1, f32[4,512]{1,0:T(4,128)} %row_moment.1, ...), custom_call_target="tpu_custom_call" | custom-call | tf_op jit(solution)/shard_map/gradients/pallas_call | solution.py:428
  131.6 5.6 %scale.1 = (f32[4,512,1024]{2,1,0:T(8,128)}, f32[4,512]{1,0:T(4,128)}, f32[4,1024]{1,0:T(4,128)}) custom-call(bf16[4,512,1024]{2,1,0:T(8,128)(2,1)} %get-tuple-element.8.code, f32[4,2,8,512]{3,2,1,0:T(8,128)} %get-tuple-element.9.left_in, f32[4,1,1024]{2,1,0:T(1,128)} %get-tuple-element.10.right_in, f32[4,512]{1,0:T(4,128)} %get-tuple-element.11.row_new, ...), custom_call_target="tpu_custom_call" | custom-call | tf_op jit(solution)/shard_map/scale/pallas_call | solution.py:475

commit v5 on v4

--- a/solution.py
+++ b/solution.py
@@ -345,9 +345,8 @@
     drain(late)
     forward(0)
     finish(2)
+    hand_on(2)
     finish(3)
-    hand_on(2)
-    hand_on(3)
 
     decay = 1.0 - float(STEP) ** (-0.8)
     tail = len(sent)
@@ -376,6 +375,7 @@
         coln[yh, p : p + 1, :] = decay * old + (1.0 - decay) * (sums[p // 2 : p // 2 + 1] / D)
     cols_new = coln[yh]
     to_cn = send(coln.at[yh], coln.at[yh], s_cn.at[0], r_cn.at[0], device(m=2))
+    hand_on(3)
     for p in range(4):
         sum1[plane_slot, 0, p : p + 1, :] = lanes(jnp.sum(rows_new[p : p + 1]) * 0.125)
         by_row = jnp.broadcast_to(1.0 / rows_new[p : p + 1], (8, TOK))

time: 139 us -> 133 us (0.957)
  Pallas kernels: 137 us -> 131 us
    pallas_call x1, Pallas kernels: 131 us -> 126 us  [gradients(): pl.pallas_call(gradient_kernel, out_shape=[jax.ShapeDtypeStruct((4, 512,...]
where the time goes in v5:
time: 133 us; the launch traced here: 132 us
  Pallas kernels  131 us (98%)
    pallas_call x1, Pallas kernels, gradients(): pl.pallas_call(gradient_kernel, out_shape=[jax.ShapeDtypeStruct((4, 512,...  126 us
    pallas_call x1, Pallas kernels, local(): pl.pallas_call(scale_kernel, out_shape=[jax.ShapeDtypeStruct((4, 512, 102...  5.62 us

profile of v5, /device:TPU:0, one launch (start us, length us, event | category | flops | bytes accessed | tf_op | source)
XLA Modules:
  0.0 132.0 jit_solution(15330150024780821286)
XLA Ops:
  0.6 125.6 %gradients.1 = (bf16[4,512,1024]{2,1,0:T(8,128)(2,1)}, f32[4,512]{1,0:T(4,128)}, f32[4,1024]{1,0:T(4,128)}, f32[4,2,8,512]{3,2,1,0:T(8,128)}, f32[4,1,1024]{2,1,0:T(1,128)}) custom-call(bf16[2,512,512]{2,1,0:T(8,128)(2,1)} %inputs.1, bf16[4,256,1024]{2,1,0:T(8,128)(2,1)} %out_grads.1, f32[4,512,1024]{2,1,0:T(8,128)} %weights.1, f32[4,512]{1,0:T(4,128)} %row_moment.1, ...), custom_call_target="tpu_custom_call" | custom-call | tf_op jit(solution)/shard_map/gradients/pallas_call | solution.py:428
  126.2 5.6 %scale.1 = (f32[4,512,1024]{2,1,0:T(8,128)}, f32[4,512]{1,0:T(4,128)}, f32[4,1024]{1,0:T(4,128)}) custom-call(bf16[4,512,1024]{2,1,0:T(8,128)(2,1)} %get-tuple-element.8.code, f32[4,2,8,512]{3,2,1,0:T(8,128)} %get-tuple-element.9.left_in, f32[4,1,1024]{2,1,0:T(1,128)} %get-tuple-element.10.right_in, f32[4,512]{1,0:T(4,128)} %get-tuple-element.11.row_new, ...), custom_call_target="tpu_custom_call" | custom-call | tf_op jit(solution)/shard_map/scale/pallas_call | solution.py:475

commit v6 on v5

--- a/solution.py
+++ b/solution.py
@@ -263,14 +263,16 @@
         pair[p].wait_recv()
         gradient = part[p, yl, mine, :] + pair_in[p]
         final[p] = gradient
+        norm = jnp.sum(gradient * gradient + 1e-30, axis=1, keepdims=True)
+        code[p] = encode(gradient * (TOP * lax.rsqrt(norm))).astype(jnp.bfloat16)
+        if p < 3:
+            hand_on(p)
         statistics(p)
         if p == 2:
             stats.append(exchange(colx, col_slot, col_peers, s_cx, r_cx))
         if p == 3:
             stats.append(exchange(rowx, row_slot, row_peers, s_rx, r_rx))
             stats.append(exchange(dcolx, dcol_slot, diagonal_peers, s_dx, r_dx))
-        norm = jnp.sum(gradient * gradient + 1e-30, axis=1, keepdims=True)
-        code[p] = encode(gradient * (TOP * lax.rsqrt(norm))).astype(jnp.bfloat16)
 
     def forward(p):
         to_y[p].wait_recv()
@@ -289,6 +291,7 @@
     send_ry(0)
     send_ly(0, 2)
     send_ry(1)
+    send_ry(2)
     send_xa(2)
     weight_sums()
     send_xb(0)
@@ -296,16 +299,15 @@
     send_z(0, 2)
     send_zf(0, 0)
     send_zf(0, 1)
+    send_ly(1, 1)
+    send_ly(1, 3)
+    send_ly(1, 2)
+    send_ry(3)
     send_xfb(0)
-    send_ry(2)
     send_xb(1)
     send_zf(0, 3)
     send_zf(0, 2)
     send_xfa(1)
-    send_ly(1, 1)
-    send_ly(1, 3)
-    send_ly(1, 2)
-    send_ry(3)
     send_z(1, 0)
     send_xfb(1)
     send_xb(2)
@@ -329,13 +331,11 @@
     send_zf(1, 3)
     drain(early // 2)
     finish(0)
-    hand_on(0)
     send_zf(1, 2)
     send_xfa(3)
     send_xfb(3)
     drain(early)
     finish(1)
-    hand_on(1)
     wait_r(2)
     late = len(sent) - 6
     compute(2)
@@ -345,7 +345,6 @@
     drain(late)
     forward(0)
     finish(2)
-    hand_on(2)
     finish(3)
 
     decay = 1.0 - float(STEP) ** (-0.8)
@@ -367,6 +366,7 @@
         old = col_moment[p : p + 1, columns(half[p])]
         coln[yh, p : p + 1, :] = decay * old + (1.0 - decay) * (sums[p // 2 : p // 2 + 1] / D)
     landed(stats[2])
+    hand_on(3)
     sums = dcolx[0]
     for k in range(1, 16):
         sums = sums + dcolx[k]
@@ -375,7 +375,6 @@
         coln[yh, p : p + 1, :] = decay * old + (1.0 - decay) * (sums[p // 2 : p // 2 + 1] / D)
     cols_new = coln[yh]
     to_cn = send(coln.at[yh], coln.at[yh], s_cn.at[0], r_cn.at[0], device(m=2))
-    hand_on(3)
     for p in range(4):
         sum1[plane_slot, 0, p : p + 1, :] = lanes(jnp.sum(rows_new[p : p + 1]) * 0.125)
         by_row = jnp.broadcast_to(1.0 / rows_new[p : p + 1], (8, TOK))

time: 133 us -> 133 us (level)
  no operation moved by 1% of the time
where the time goes in v6:
time: 133 us; the launch traced here: 132 us
  Pallas kernels  131 us (98%)
    pallas_call x1, Pallas kernels, gradients(): pl.pallas_call(gradient_kernel, out_shape=[jax.ShapeDtypeStruct((4, 512,...  125 us
    pallas_call x1, Pallas kernels, local(): pl.pallas_call(scale_kernel, out_shape=[jax.ShapeDtypeStruct((4, 512, 102...  5.62 us

profile of v6, /device:TPU:0, one launch (start us, length us, event | category | flops | bytes accessed | tf_op | source)
XLA Modules:
  0.0 131.7 jit_solution(1480052522415699435)
XLA Ops:
  0.6 125.3 %gradients.1 = (bf16[4,512,1024]{2,1,0:T(8,128)(2,1)}, f32[4,512]{1,0:T(4,128)}, f32[4,1024]{1,0:T(4,128)}, f32[4,2,8,512]{3,2,1,0:T(8,128)}, f32[4,1,1024]{2,1,0:T(1,128)}) custom-call(bf16[2,512,512]{2,1,0:T(8,128)(2,1)} %inputs.1, bf16[4,256,1024]{2,1,0:T(8,128)(2,1)} %out_grads.1, f32[4,512,1024]{2,1,0:T(8,128)} %weights.1, f32[4,512]{1,0:T(4,128)} %row_moment.1, ...), custom_call_target="tpu_custom_call" | custom-call | tf_op jit(solution)/shard_map/gradients/pallas_call | solution.py:427
  125.9 5.6 %scale.1 = (f32[4,512,1024]{2,1,0:T(8,128)}, f32[4,512]{1,0:T(4,128)}, f32[4,1024]{1,0:T(4,128)}) custom-call(bf16[4,512,1024]{2,1,0:T(8,128)(2,1)} %get-tuple-element.8.code, f32[4,2,8,512]{3,2,1,0:T(8,128)} %get-tuple-element.9.left_in, f32[4,1,1024]{2,1,0:T(1,128)} %get-tuple-element.10.right_in, f32[4,512]{1,0:T(4,128)} %get-tuple-element.11.row_new, ...), custom_call_target="tpu_custom_call" | custom-call | tf_op jit(solution)/shard_map/scale/pallas_call | solution.py:474
